TPU v7x, 256 devices: a whole 4x4x8 slice. The times are simulated.
256 devices in a mesh: row: 8 (over z_lo, core), col: 8 (over x, z_hi), depth: 4 (over y).
Axes of the slice: x: 4, y: 4, z: 8 (z_hi: 2, z_lo: 4; z = z_hi * 4 + z_lo), core: 2. Of those that a mesh axis runs over, the one named last changes fastest.
Arguments:
- tokens: bfloat16 [5120, 8192], P(('row', 'depth'), 'col'), may hold values from -6 to 6
- weight: bfloat16 [8192, 4096], P('row', 'col'), may hold values from -0.0625 to 0.0625
- cotangent: bfloat16 [5120, 4096], P(('row', 'depth'), 'col'), may hold values from -6 to 6
- master: float32 [8192, 4096], P(('row', 'depth'), 'col'), may hold values from -0.1 to 0.1
- first_moment: float32 [8192, 4096], P(('row', 'depth'), 'col'), may hold values from -6 to 6
- second_moment: float32 [8192, 4096], P(('row', 'depth'), 'col'), may hold values from 0.1 to 10
Outputs:
- queries: bfloat16 [5120, 4096], P(('row', 'depth'), 'col')
- token_grad: bfloat16 [5120, 8192], P(('row', 'depth'), 'col')
- new_master: float32 [8192, 4096], P(('row', 'depth'), 'col')
- new_first: float32 [8192, 4096], P(('row', 'depth'), 'col')
- new_second: float32 [8192, 4096], P(('row', 'depth'), 'col')
- new_weight: bfloat16 [8192, 4096], P('row', 'col')
All inputs are finite; a program needn't handle non-finite values.
Results may differ from a plain program's by a relative error of at most 0.001.
Values may be sent and summed in bfloat16 or wider, within the bound.
No kernel may reach another device: no remote copies, remote signals or barrier semaphores. Data moves between devices by JAX's collectives and lax.ppermute only.
A program may use at most 128 MiB of HBM per device.

v0:
```python
import math

import jax
import jax.numpy as jnp
from jax import lax
from jax.sharding import PartitionSpec as P

beta_one = 0.9
beta_two = 0.95
learn_rate = 0.02
decay_rate = 0.1
adam_eps = 1e-08
bias_one = 1.0 - 0.9**50
bias_two = 1.0 - 0.95**50


def local(tokens, weight, cotangent, master, first_moment, second_moment):
    total_tokens = tokens.shape[0] * lax.axis_size("row") * lax.axis_size("depth")
    grad_scale = 1.0 / math.sqrt(total_tokens)
    full_rows = lax.all_gather(tokens, "col", axis=1, tiled=True)
    full_panel = lax.all_gather(weight, "row", axis=0, tiled=True)
    queries = jnp.dot(full_rows, full_panel, preferred_element_type=jnp.float32).astype(
        jnp.bfloat16
    )
    partial_value = lax.dot_general(
        cotangent, full_panel, (((1,), (1,)), ((), ())), preferred_element_type=jnp.float32
    )
    token_grad = lax.psum_scatter(partial_value, "col", scatter_dimension=1, tiled=True).astype(
        jnp.bfloat16
    )
    product = lax.dot_general(
        full_rows, cotangent, (((0,), (0,)), ((), ())), preferred_element_type=jnp.float32
    )
    grad = lax.psum_scatter(product * grad_scale, ("row", "depth"), scatter_dimension=0, tiled=True)
    new_first = beta_one * first_moment + (1.0 - beta_one) * grad
    new_second = beta_two * second_moment + (1.0 - beta_two) * grad * grad
    step_value = new_first / bias_one / (jnp.sqrt(new_second / bias_two) + adam_eps)
    new_master = master - learn_rate * (step_value + decay_rate * master)
    shard_weight = new_master.astype(jnp.bfloat16)
    new_weight = lax.all_gather(shard_weight, "depth", axis=0, tiled=True)
    return (queries, token_grad, new_master, new_first, new_second, new_weight)


def solution(mesh):
    in_specs = (
        P(("row", "depth"), "col"),
        P("row", "col"),
        P(("row", "depth"), "col"),
        P(("row", "depth"), "col"),
        P(("row", "depth"), "col"),
        P(("row", "depth"), "col"),
    )
    out_specs = (
        P(("row", "depth"), "col"),
        P(("row", "depth"), "col"),
        P(("row", "depth"), "col"),
        P(("row", "depth"), "col"),
        P(("row", "depth"), "col"),
        P("row", "col"),
    )
    return jax.shard_map(local, mesh=mesh, in_specs=in_specs, out_specs=out_specs, check_vma=False)
```

profile of v0, /device:TPU:2, one launch (start us, length us, event | category | flops | bytes accessed | tf_op | source)
XLA Modules:
  0.0 557.0 jit_solution(13067919387536459166)
XLA Ops:
  7.2 0.0 copy-start
  7.2 0.0 all-gather.4.cloned.1.call-start
  7.2 0.7 all-gather.4.cloned.1.call-update
  7.9 0.0 all-gather.6.cloned.1.call-start
  8.0 0.7 all-gather.6.cloned.1.call-update
  8.7 0.0 reduce-scatter.5.cloned.1.call-start
  8.7 88.3 %all-gather.4.cloned.1.call-done = bf16[160,8192]{1,0:T(8,128)(2,1)} async-done(((bf16[160,1024]{1,0:T(8,128)(2,1)}), bf16[160,8192]{1,0:T(8,128)(2,1)}) %all-gather.4.cloned.1.call-update) | async-done | bytes 2621456 | tf_op jit(solution)/shard_map/all_gather | solution.py:20
  97.0 0.0 copy-done
  97.0 10.1 %convolution_multiply_fusion = f32[8192,512]{1,0:T(8,128)} fusion(bf16[160,8192]{1,0:T(8,128)(2,1)} %all-gather.4.cloned.1.call-done, bf16[160,512]{1,0:T(8,128)(2,1)S(1)} %copy-done), kind=kOutput, calls=%fused_computation | convolution fusion | flops 1346371584 | bytes 19562496 | tf_op jit(solution)/shard_map/dot_general | solution.py:31
  107.1 0.0 reduce-scatter.5.cloned.1.call-update
  107.1 0.0 copy-start.2
  107.1 0.0 copy-start.1
  107.1 0.0 reduce-scatter.3.cloned.1.call-start
  107.1 81.5 %all-gather.6.cloned.1.call-done = bf16[8192,512]{1,0:T(8,128)(2,1)} async-done(((bf16[1024,512]{1,0:T(8,128)(2,1)}), bf16[8192,512]{1,0:T(8,128)(2,1)}) %all-gather.6.cloned.1.call-update) | async-done | bytes 8388624 | tf_op jit(solution)/shard_map/all_gather | solution.py:21
  188.7 8.7 %fusion.3 = f32[160,8192]{1,0:T(8,128)} fusion(bf16[160,512]{1,0:T(8,128)(2,1)S(1)} %copy-done, bf16[8192,512]{1,0:T(8,128)(2,1)} %all-gather.6.cloned.1.call-done), kind=kOutput, calls=%fused_computation.7 | convolution fusion | flops 1342177280 | bytes 13795328 | tf_op jit(solution)/shard_map/dot_general | solution.py:25
  197.4 0.0 reduce-scatter.3.cloned.1.call-update
  197.4 0.0 all-gather.8.cloned.1.call-start
  197.4 180.7 %reduce-scatter.5.cloned.1.call-done = f32[256,512]{1,0:T(8,128)} async-done(((f32[8192,512]{1,0:T(8,128)}), f32[256,512]{1,0:T(8,128)}) %reduce-scatter.5.cloned.1.call-update) | async-done | bytes 524304 | tf_op jit(solution)/shard_map/reduce_scatter | solution.py:34
  378.2 0.0 copy-done.2
  378.2 2.9 fusion.1
  381.0 0.0 all-gather.8.cloned.1.call-update
  381.1 0.0 copy-done.1
  381.1 5.6 %convolution_convert_fusion = bf16[160,512]{1,0:T(8,128)(2,1)} fusion(bf16[160,8192]{1,0:T(8,128)(2,1)S(1)} %copy-done.1, bf16[8192,512]{1,0:T(8,128)(2,1)} %all-gather.6.cloned.1.call-done), kind=kOutput, calls=%fused_computation.1 | convolution fusion | flops 1342259200 | bytes 11173888 | tf_op jit(solution)/shard_map/dot_general | solution.py:22
  386.6 136.7 %reduce-scatter.3.cloned.1.call-done = f32[160,1024]{1,0:T(8,128)} async-done(((f32[160,8192]{1,0:T(8,128)}), f32[160,1024]{1,0:T(8,128)}) %reduce-scatter.3.cloned.1.call-update) | async-done | bytes 655376 | tf_op jit(solution)/shard_map/reduce_scatter | solution.py:28
  523.3 1.9 convert_element_type.10
  525.2 23.0 %all-gather.8.cloned.1.call-done = bf16[1024,512]{1,0:T(8,128)(2,1)} async-done(((bf16[256,512]{1,0:T(8,128)(2,1)}), bf16[1024,512]{1,0:T(8,128)(2,1)}) %all-gather.8.cloned.1.call-update) | async-done | bytes 1048592 | tf_op jit(solution)/shard_map/all_gather | solution.py:40
  548.2 2.3 copy.13
Async XLA Ops:
  7.2 89.8 %copy-start = (bf16[160,512]{1,0:T(8,128)(2,1)S(1)}, bf16[160,512]{1,0:T(8,128)(2,1)}, u32[]{:S(2)}) copy-start(bf16[160,512]{1,0:T(8,128)(2,1)} %param.8) | copy-start | bytes 491524
  7.2 89.8 %all-gather.4.cloned.1.call-start = ((), (), s32[]{:S(2)}) async-start(), calls=%async_computation.2 | async-start | bytes 2949120 | tf_op jit(solution)/shard_map/all_gather | solution.py:20
  7.9 180.8 %all-gather.6.cloned.1.call-start = ((), (), s32[]{:S(2)}) async-start(), calls=%async_computation.3 | async-start | bytes 9437184 | tf_op jit(solution)/shard_map/all_gather | solution.py:21
  8.7 369.5 %reduce-scatter.5.cloned.1.call-start = ((), (), s32[]{:S(2)}) async-start(), calls=%async_computation.5 | async-start | bytes 17301504 | tf_op jit(solution)/shard_map/reduce_scatter | solution.py:34
  107.1 271.1 %copy-start.2 = (f32[256,512]{1,0:T(8,128)S(1)}, f32[256,512]{1,0:T(8,128)}, u32[]{:S(2)}) copy-start(f32[256,512]{1,0:T(8,128)} %param.9) | copy-start | bytes 1572868
  107.1 274.0 %copy-start.1 = (bf16[160,8192]{1,0:T(8,128)(2,1)S(1)}, bf16[160,8192]{1,0:T(8,128)(2,1)}, u32[]{:S(2)}) copy-start(bf16[160,8192]{1,0:T(8,128)(2,1)} %all-gather.4.cloned.1.call-done) | copy-start | bytes 7864324
  107.1 416.2 %reduce-scatter.3.cloned.1.call-start = ((), (), s32[]{:S(2)}) async-start(), calls=%async_computation.4 | async-start | bytes 5898240 | tf_op jit(solution)/shard_map/reduce_scatter | solution.py:28
  197.4 350.8 %all-gather.8.cloned.1.call-start = ((), (), s32[]{:S(2)}) async-start(), calls=%async_computation.6 | async-start | bytes 1310720 | tf_op jit(solution)/shard_map/all_gather | solution.py:40
Sparse Core Ops, SparseCore 0:
  10.7 86.2 all-gather.3
  98.8 89.8 all-gather.5
  191.2 186.8 reduce-scatter.4
  382.2 141.0 reduce-scatter.2
  525.7 22.4 all-gather.7
where the time goes:
time: 557 us
  waiting for transfers between devices  512 us (92%)
  matrix products  24.3 us (4%)
  between operations  13.8 us (2%)
    reduce_scatter x1, waiting for transfers between devices, local(): lax.psum_scatter(product * grad_scale, ('row', 'depth'), scatter_dimensio...  181 us
    reduce_scatter x1, waiting for transfers between devices, local(): lax.psum_scatter(partial_value, 'col', scatter_dimension=1, tiled=True)  137 us
    all_gather x1, waiting for transfers between devices, local(): full_rows = lax.all_gather(tokens, 'col', axis=1, tiled=True)  88.3 us
    all_gather x1, waiting for transfers between devices, local(): full_panel = lax.all_gather(weight, 'row', axis=0, tiled=True)  81.5 us
    all_gather x1, waiting for transfers between devices, local(): new_weight = lax.all_gather(shard_weight, 'depth', axis=0, tiled=True)  23 us
  transfers between devices with their start and end apart: 5, of which 5 were waited for; matrix products, arithmetic and copies ran while one was open for 5% of the time, Pallas kernels for 0%

commit v1 on v0

v1 whole, which is shorter than its diff:
```python
import math

import jax
import jax.numpy as jnp
from jax import lax
from jax.sharding import PartitionSpec as P

beta_one = 0.9
beta_two = 0.95
learn_rate = 0.02
decay_rate = 0.1
adam_eps = 1e-08
bias_one = 1.0 - 0.9**50
bias_two = 1.0 - 0.95**50

AXES = ("row", "col", "depth")
f32 = jnp.float32
bf16 = jnp.bfloat16


def moves(sizes, change):
    rows, cols, depths = sizes
    pairs = []
    for r in range(rows):
        for c in range(cols):
            for y in range(depths):
                zlo, core, x, zhi, yy = change(r // 2, r % 2, c // 2, c % 2, y)
                pairs.append(
                    (
                        (r * cols + c) * depths + y,
                        ((zlo * 2 + core) * cols + x * 2 + zhi) * depths + yy,
                    )
                )
    return pairs


def local(tokens, weight, cotangent, master, first_moment, second_moment):
    sizes = tuple(lax.axis_size(a) for a in AXES)
    nz, nx, ny = sizes[0] // 2, sizes[1] // 2, sizes[2]
    total_tokens = tokens.shape[0] * sizes[0] * sizes[2]
    grad_scale = 1.0 / math.sqrt(total_tokens)

    def send(value, change):
        return lax.ppermute(value, AXES, moves(sizes, change))

    def flip(value):
        return send(value, lambda zlo, core, x, zhi, y: (x, zhi, zlo, core, y))

    def along_x(value, step):
        return send(value, lambda zlo, core, x, zhi, y: (zlo, core, (x + step) % nx, zhi, y))

    def along_z(value, step):
        return send(value, lambda zlo, core, x, zhi, y: ((zlo + step) % nz, core, x, zhi, y))

    def other_core(value):
        return send(value, lambda zlo, core, x, zhi, y: (zlo, 1 - core, x, zhi, y))

    def other_zhi(value):
        return send(value, lambda zlo, core, x, zhi, y: (zlo, core, x, 1 - zhi, y))

    row, col, y = (lax.axis_index(a) for a in AXES)
    zlo, core, x, zhi = row // 2, row % 2, col // 2, col % 2

    def over_col(value):
        far = other_zhi(value)
        pair = jnp.where(zhi == 0, jnp.stack([value, far]), jnp.stack([far, value]))
        left, right = along_x(pair, 1), along_x(pair, -1)
        across = jnp.stack([along_x(left[0], 1), along_x(right[1], -1)])
        whole = jnp.zeros((nx,) + pair.shape, pair.dtype)
        for step, block in ((0, pair), (1, left), (2, across), (3, right)):
            whole = lax.dynamic_update_index_in_dim(whole, block, (x - step) % nx, 0)
        return whole

    quarter = weight.shape[0] // ny
    part = lax.dynamic_slice_in_dim(weight, y * quarter, quarter, 0)

    turned_tokens = lax.all_to_all(flip(tokens), "depth", 1, 0, tiled=True)
    turned_part = flip(part)
    cot_parts = [cotangent] + [along_z(cotangent, s) for s in range(1, nz)]
    both = jnp.stack([part, turned_part])
    parts = [turned_part] + [along_z(both, s) for s in range(1, nz)]

    wide = over_col(jnp.concatenate([tokens, cotangent], axis=1))
    features = tokens.shape[1]
    turned = over_col(turned_tokens)

    def select(buffer, zl, co):
        return lax.dynamic_slice(
            buffer, (zl, co) + (0,) * (buffer.ndim - 2), (1, 1) + buffer.shape[2:]
        ).reshape(buffer.shape[2:])

    grad = 0.0
    for s in range(nz):
        mine = lax.all_gather(cot_parts[s], "depth", axis=0, tiled=True)
        theirs = other_core(mine)
        zl = (zlo - s) % nz
        for co, block in ((core, mine), (1 - core, theirs)):
            grad += lax.dot_general(
                select(turned, zl, co), block, (((0,), (0,)), ((), ())), preferred_element_type=f32
            )
    grad = grad * grad_scale
    new_first = beta_one * first_moment + (1.0 - beta_one) * grad
    new_second = beta_two * second_moment + (1.0 - beta_two) * grad * grad
    step_value = new_first / bias_one / (jnp.sqrt(new_second / bias_two) + adam_eps)
    new_master = master - learn_rate * (step_value + decay_rate * master)
    shard_weight = new_master.astype(bf16)
    new_weight = lax.all_gather(shard_weight, "depth", axis=0, tiled=True)

    queries = 0.0
    token_grad = 0.0
    for s in range(nz):
        gathered = lax.all_gather(parts[s], "depth", axis=0, tiled=False)
        if s == 0:
            mine = (weight, gathered.reshape(weight.shape))
            theirs = tuple(other_core(m) for m in mine)
        else:
            swapped = other_core(gathered)
            mine, theirs = (
                tuple(v[:, i].reshape(weight.shape) for i in range(2)) for v in (gathered, swapped)
            )
        zl = (zlo - s) % nz
        for co, (plain, turn) in ((core, mine), (1 - core, theirs)):
            block = select(wide, zl, co)
            queries += jnp.dot(block[:, :features], plain, preferred_element_type=f32)
            token_grad += lax.dot_general(
                block[:, features:], turn, (((1,), (1,)), ((), ())), preferred_element_type=f32
            )
    return (
        queries.astype(bf16),
        token_grad.astype(bf16),
        new_master,
        new_first,
        new_second,
        new_weight,
    )


def solution(mesh):
    in_specs = (
        P(("row", "depth"), "col"),
        P("row", "col"),
        P(("row", "depth"), "col"),
        P(("row", "depth"), "col"),
        P(("row", "depth"), "col"),
        P(("row", "depth"), "col"),
    )
    out_specs = (
        P(("row", "depth"), "col"),
        P(("row", "depth"), "col"),
        P(("row", "depth"), "col"),
        P(("row", "depth"), "col"),
        P(("row", "depth"), "col"),
        P("row", "col"),
    )
    return jax.shard_map(local, mesh=mesh, in_specs=in_specs, out_specs=out_specs, check_vma=False)
```

time: 557 us -> 304 us (0.55)
  waiting for transfers between devices: 512 us -> 139 us
  blocking collectives: 0 us -> 54.9 us
  starting transfers between devices: 0.2 us -> 34.8 us
  local copies, waits for them, and re-layouts: 2.28 us -> 30.4 us
    reduce_scatter x2 -> x0, waiting for transfers between devices: 317 us -> none  [the longest x1 181 us: local(): lax.psum_scatter(product * grad_scale, ('row', 'depth'), scatter_dimensio...]
    all_gather x2 -> x4, waiting for transfers between devices: 170 us -> 14 us  [local(): gathered = lax.all_gather(parts[s], 'depth', axis=0, tiled=False)]
    ppermute x0 -> x27, waiting for transfers between devices: none -> 122 us  [send(): return lax.ppermute(value, AXES, moves(sizes, change))]
    all_gather x0 -> x4, blocking collectives: none -> 54.9 us  [local(): mine = lax.all_gather(cot_parts[s], 'depth', axis=0, tiled=True)]
    ppermute x0 -> x27, starting transfers between devices: none -> 30.2 us  [send(): return lax.ppermute(value, AXES, moves(sizes, change))]
    all_gather x1, waiting for transfers between devices: 23 us -> 0.01 us  [local(): new_weight = lax.all_gather(shard_weight, 'depth', axis=0, tiled=True)]
    slice x0 -> x6, local copies, waits for them, and re-layouts: none -> 6.98 us  [local(): v[:, i].reshape(weight.shape)]
    dot_general x3 -> x24, matrix products: 24.3 us -> 21.3 us  [the longest x8 8.4 us: local(): lax.dot_general(block[:, features:], turn, (((1,), (1,)), ((), ())), pref...]
  transfers between devices with their start and end apart: 5 -> 33, of which waited for: 5 -> 13; matrix products, arithmetic and copies ran while one was open for 5% -> 15% of each run, Pallas kernels for 0% -> 0%
where the time goes in v1:
time: 304 us; the launch traced here: 301 us
  waiting for transfers between devices  139 us (46%)
  blocking collectives  54.9 us (18%)
  starting transfers between devices  34.8 us (11%)
  local copies, waits for them, and re-layouts  30.4 us (10%)
  matrix products  21.3 us (7%)
  between operations  14.3 us (5%)
  other arithmetic  6.43 us (2%)
    ppermute x27, waiting for transfers between devices, send(): return lax.ppermute(value, AXES, moves(sizes, change))  122 us
    all_gather x4, blocking collectives, local(): mine = lax.all_gather(cot_parts[s], 'depth', axis=0, tiled=True)  54.9 us
    ppermute x27, starting transfers between devices, send(): return lax.ppermute(value, AXES, moves(sizes, change))  30.2 us
    all_gather x4, waiting for transfers between devices, local(): gathered = lax.all_gather(parts[s], 'depth', axis=0, tiled=False)  14 us
    dot_general x8, matrix products, local(): lax.dot_general(block[:, features:], turn, (((1,), (1,)), ((), ())), pref...  8.4 us
    dot_general x8, matrix products, local(): lax.dot_general(select(turned, zl, co), block, (((0,), (0,)), ((), ())),...  8.22 us
    slice x6, local copies, waits for them, and re-layouts, local(): v[:, i].reshape(weight.shape)  6.98 us
    unnamed x52, local copies, waits for them, and re-layouts  6.86 us
  transfers between devices with their start and end apart: 33, of which 13 were waited for; matrix products, arithmetic and copies ran while one was open for 15% of the time, Pallas kernels for 0%

profile of v1, /device:TPU:2, one launch (start us, length us, event | category | flops | bytes accessed | tf_op | source)
XLA Modules:
  0.0 301.3 jit_solution(17373381705395759390)
XLA Ops:
  7.2 3.8 %collective-permute-start.14 = (bf16[160,1024]{1,0:T(8,128)(2,1)}, bf16[160,1024]{1,0:T(8,128)(2,1)S(1)}, u32[]{:S(2)}, u32[]{:S(2)}) collective-permute-start(bf16[160,1024]{1,0:T(8,128)(2,1)} %param.6), channel_id=1, source_target_pairs={{0,0},{1,1},{2,2},{3,3},{4,32},{5,33},{6,34},{7,35},{8,64},{9,65},... | collective-permute-start | bytes 983048 | tf_op jit(solution)/shard_map/ppermute | solution.py:44
  11.0 16.8 %collective-permute-done.14 = bf16[160,1024]{1,0:T(8,128)(2,1)S(1)} collective-permute-done((bf16[160,1024]{1,0:T(8,128)(2,1)}, bf16[160,1024]{1,0:T(8,128)(2,1)S(1)}, u32[]{:S(2)}, u32[]{:S(2)}) %collective-permute-start.14) | collective-permute-done | bytes 327712 | tf_op jit(solution)/shard_map/ppermute | solution.py:44
  27.8 0.7 copy.18
  28.5 4.5 %all-to-all-start = ((bf16[160,4,256]{2,0,1:T(8,128)(2,1)}), bf16[160,4,256]{2,0,1:T(8,128)(2,1)S(1)}, u32[]{:S(2)}, u32[]{:S(2)}) async-start(bf16[160,4,256]{2,0,1:T(8,128)(2,1)} %bitcast.128), calls=%async_computation | async-start | bytes 655360 | tf_op jit(solution)/shard_map/all_to_all | solution.py:77
  33.0 3.3 %collective-permute-start.25 = (bf16[160,512]{1,0:T(8,128)(2,1)}, bf16[160,512]{1,0:T(8,128)(2,1)S(1)}, u32[]{:S(2)}, u32[]{:S(2)}) collective-permute-start(bf16[160,512]{1,0:T(8,128)(2,1)} %param.8), channel_id=1, source_target_pairs={{0,192},{1,193},{2,194},{3,195},{4,196},{5,197},{6,198},{7,199},{8... | collective-permute-start | bytes 491528 | tf_op jit(solution)/shard_map/ppermute | solution.py:44
  37.0 3.1 %all-to-all-done = bf16[160,4,256]{2,0,1:T(8,128)(2,1)S(1)} async-done(((bf16[160,4,256]{2,0,1:T(8,128)(2,1)}), bf16[160,4,256]{2,0,1:T(8,128)(2,1)S(1)}, u32[]{:S(2)}, u32[]{:S(2)}) %all-to-all-start) | async-done | bytes 327712 | tf_op jit(solution)/shard_map/all_to_all | solution.py:77
  40.0 5.9 %collective-permute-start.15 = (bf16[640,256]{1,0:T(8,128)(2,1)S(1)}, bf16[640,256]{1,0:T(8,128)(2,1)S(1)}, u32[]{:S(2)}, u32[]{:S(2)}) collective-permute-start(bf16[640,256]{1,0:T(8,128)(2,1)S(1)} %bitcast.143), channel_id=1, source_target_pairs={{0,4},{1,5},{2,6},{3,7},{4,0},{5,1},{6,2},{7,3},{8,12},{9,13},{10,... | collective-permute-start | bytes 983048 | tf_op jit(solution)/shard_map/ppermute | solution.py:44
  46.0 1.7 constant_dynamic-slice_fusion
  47.6 3.0 %collective-permute-start.6 = (bf16[256,512]{1,0:T(8,128)(2,1)}, bf16[256,512]{1,0:T(8,128)(2,1)S(1)}, u32[]{:S(2)}, u32[]{:S(2)}) collective-permute-start(bf16[256,512]{1,0:T(8,128)(2,1)} %constant_dynamic-slice_fusion), channel_id=1, source_target_pairs={{0,0},{1,1},{2,2},{3,3},{4,32},{5,33},{6,34},{7,35},{8,64},{9,65},... | collective-permute-start | bytes 786440 | tf_op jit(solution)/shard_map/ppermute | solution.py:44
  50.7 13.4 %all_gather.44 = bf16[640,512]{1,0:T(8,128)(2,1)S(1)} all-gather(bf16[160,512]{1,0:T(8,128)(2,1)} %param.8), channel_id=1, replica_groups=mesh['row'=8,'col'=8,'depth'=4] {'depth'}, dimensions={0}, use_global_device_ids=true | all-gather | bytes 819200 | tf_op jit(solution)/shard_map/all_gather | solution.py:94
  64.1 10.2 %collective-permute-done.15 = bf16[640,256]{1,0:T(8,128)(2,1)S(1)} collective-permute-done((bf16[640,256]{1,0:T(8,128)(2,1)S(1)}, bf16[640,256]{1,0:T(8,128)(2,1)S(1)}, u32[]{:S(2)}, u32[]{:S(2)}) %collective-permute-start.15) | collective-permute-done | bytes 327712 | tf_op jit(solution)/shard_map/ppermute | solution.py:44
  74.3 0.9 maximum_select_fusion.3
  75.2 14.0 %all_gather.47 = bf16[640,512]{1,0:T(8,128)(2,1)S(1)} all-gather(bf16[160,512]{1,0:T(8,128)(2,1)S(1)} %collective-permute-done.25), channel_id=1, replica_groups=mesh['row'=8,'col'=8,'depth'=4] {'depth'}, dimensions={0}, use_global_device_ids=true | all-gather | bytes 819200 | tf_op jit(solution)/shard_map/all_gather | solution.py:94
  89.3 1.7 collective-permute-start.16
  91.0 13.8 %all_gather.46 = bf16[640,512]{1,0:T(8,128)(2,1)S(1)} all-gather(bf16[160,512]{1,0:T(8,128)(2,1)S(1)} %collective-permute-done.23), channel_id=1, replica_groups=mesh['row'=8,'col'=8,'depth'=4] {'depth'}, dimensions={0}, use_global_device_ids=true | all-gather | bytes 819200 | tf_op jit(solution)/shard_map/all_gather | solution.py:94
  105.5 13.7 %all_gather.45 = bf16[640,512]{1,0:T(8,128)(2,1)S(1)} all-gather(bf16[160,512]{1,0:T(8,128)(2,1)} %copy-done.24), channel_id=1, replica_groups=mesh['row'=8,'col'=8,'depth'=4] {'depth'}, dimensions={0}, use_global_device_ids=true | all-gather | bytes 819200 | tf_op jit(solution)/shard_map/all_gather | solution.py:94
  120.0 1.0 slice_bitcast_fusion.2
  121.3 1.0 slice_bitcast_fusion.3
  122.3 1.8 collective-permute-start.17
  124.5 1.1 bitcast_dynamic-update-slice_fusion.3
  125.6 5.0 %collective-permute-done.19 = bf16[640,256]{1,0:T(8,128)(2,1)S(1)} collective-permute-done((bf16[640,256]{1,0:T(8,128)(2,1)S(1)}, bf16[640,256]{1,0:T(8,128)(2,1)S(1)}, u32[]{:S(2)}, u32[]{:S(2)}) %collective-permute-start.19) | collective-permute-done | bytes 327712 | tf_op jit(solution)/shard_map/ppermute | solution.py:44
  130.5 1.2 collective-permute-done.17
  131.8 1.1 bitcast_dynamic-update-slice_fusion.2
  133.8 1.5 fusion.27
  135.3 1.5 fusion.31
  137.2 1.5 fusion.38
  139.2 2.2 fusion.69
  141.5 0.9 pad_maximum_fusion
  142.4 24.0 %collective-permute-done.9 = bf16[2,256,512]{2,1,0:T(8,128)(2,1)S(1)} collective-permute-done((bf16[2,256,512]{2,1,0:T(8,128)(2,1)}, bf16[2,256,512]{2,1,0:T(8,128)(2,1)S(1)}, u32[]{:S(2)}, u32[]{:S(2)}) %collective-permute-start.9) | collective-permute-done | bytes 524320 | tf_op jit(solution)/shard_map/ppermute | solution.py:44
  166.4 0.8 copy-done.20
  167.3 1.9 collective-permute-start.11
  169.2 12.4 %collective-permute-done.11 = bf16[2,256,512]{2,1,0:T(8,128)(2,1)S(1)} collective-permute-done((bf16[2,256,512]{2,1,0:T(8,128)(2,1)}, bf16[2,256,512]{2,1,0:T(8,128)(2,1)S(1)}, u32[]{:S(2)}, u32[]{:S(2)}) %collective-permute-start.11) | collective-permute-done | bytes 524320 | tf_op jit(solution)/shard_map/ppermute | solution.py:44
  181.6 0.8 copy-done.21
  182.5 3.0 collective-permute-start
  185.5 24.1 %collective-permute-done = bf16[160,1536]{1,0:T(8,128)(2,1)S(1)} collective-permute-done((bf16[160,1536]{1,0:T(8,128)(2,1)S(1)}, bf16[160,1536]{1,0:T(8,128)(2,1)S(1)}, u32[]{:S(2)}, u32[]{:S(2)}) %collective-permute-start) | collective-permute-done | bytes 491552 | tf_op jit(solution)/shard_map/ppermute | solution.py:44
  209.6 1.1 maximum_select_fusion.1
  210.7 1.9 collective-permute-start.3
  212.8 2.2 broadcast_in_dim.28
  215.0 1.1 fusion.12
  216.2 10.4 %collective-permute-done.7 = bf16[2,256,512]{2,1,0:T(8,128)(2,1)S(1)} collective-permute-done((bf16[2,256,512]{2,1,0:T(8,128)(2,1)}, bf16[2,256,512]{2,1,0:T(8,128)(2,1)S(1)}, u32[]{:S(2)}, u32[]{:S(2)}) %collective-permute-start.7) | collective-permute-done | bytes 524320 | tf_op jit(solution)/shard_map/ppermute | solution.py:44
  226.5 0.8 copy-done.22
  227.4 6.1 %collective-permute-done.3 = bf16[2,160,1536]{2,1,0:T(8,128)(2,1)S(1)} collective-permute-done((bf16[2,160,1536]{2,1,0:T(8,128)(2,1)}, bf16[2,160,1536]{2,1,0:T(8,128)(2,1)S(1)}, u32[]{:S(2)}, u32[]{:S(2)}) %collective-permute-start.3) | collective-permute-done | bytes 983072 | tf_op jit(solution)/shard_map/ppermute | solution.py:44
  233.5 0.8 slice_bitcast_fusion
  234.3 1.4 collective-permute-start.4
  235.7 0.8 slice_bitcast_fusion.1
  237.2 1.1 bitcast_dynamic-update-slice_fusion.1
  238.2 8.6 %collective-permute-done.4 = bf16[160,1536]{1,0:T(8,128)(2,1)} collective-permute-done((bf16[160,1536]{1,0:T(8,128)(2,1)}, bf16[160,1536]{1,0:T(8,128)(2,1)}, u32[]{:S(2)}, u32[]{:S(2)}) %collective-permute-start.4) | collective-permute-done | bytes 491552 | tf_op jit(solution)/shard_map/ppermute | solution.py:44
  246.9 3.1 %collective-permute-done.2 = bf16[160,1536]{1,0:T(8,128)(2,1)} collective-permute-done((bf16[160,1536]{1,0:T(8,128)(2,1)}, bf16[160,1536]{1,0:T(8,128)(2,1)}, u32[]{:S(2)}, u32[]{:S(2)}) %collective-permute-start.2) | collective-permute-done | bytes 491552 | tf_op jit(solution)/shard_map/ppermute | solution.py:44
  250.0 2.2 fusion.13
  252.2 1.0 bitcast_dynamic-update-slice_fusion
  253.2 3.7 %dynamic-slice_bitcast_fusion = (bf16[160,1536]{1,0:T(8,128)(2,1)}, bf16[160,1536]{1,0:T(8,128)(2,1)}, bf16[160,1536]{1,0:T(8,128)(2,1)}, bf16[160,1536]{1,0:T(8...) fusion(bf16[4,2,160,1536]{3,2,1,0:T(8,128)(2,1)} %bitcast_dynam, ...), kind=kLoop, calls=%fused_computation.43 | loop fusion | bytes 7864344 | tf_op jit(solution)/shard_map/reshape | solution.py:90
  257.7 1.7 convolution_add_fusion.10
  259.4 1.3 fusion.58
  261.2 2.8 fusion.75
  264.3 14.0 %all-gather.12.cloned.1.call-done = bf16[8,256,512]{2,1,0:T(8,128)(2,1)} async-done(((bf16[2,256,512]{2,1,0:T(8,128)(2,1)}), bf16[8,256,512]{2,1,0:T(8,128)(2,1)}) %all-gather.12.cloned.1.call-update) | async-done | bytes 2097168 | tf_op jit(solution)/shard_map/all_gather | solution.py:112
  278.3 1.6 fusion.50
  279.8 1.4 fusion.53
  283.7 1.4 fusion.2
  285.3 0.9 copy-done.7
  286.5 1.8 fusion.71
  288.8 1.8 fusion.70
  290.6 1.0 fusion.11
  292.6 1.2 fusion.8
  293.8 1.0 copy.29
  (115 shorter events, 11.4 us)
Async XLA Ops:
  7.2 20.6 %collective-permute-start.14 = (bf16[160,1024]{1,0:T(8,128)(2,1)}, bf16[160,1024]{1,0:T(8,128)(2,1)S(1)}, u32[]{:S(2)}, u32[]{:S(2)}) collective-permute-start(bf16[160,1024]{1,0:T(8,128)(2,1)} %param.6), channel_id=1, source_target_pairs={{0,0},{1,1},{2,2},{3,3},{4,32},{5,33},{6,34},{7,35},{8,64},{9,65},... | collective-permute-start | bytes 983048 | tf_op jit(solution)/shard_map/ppermute | solution.py:44
  28.5 11.5 %all-to-all-start = ((bf16[160,4,256]{2,0,1:T(8,128)(2,1)}), bf16[160,4,256]{2,0,1:T(8,128)(2,1)S(1)}, u32[]{:S(2)}, u32[]{:S(2)}) async-start(bf16[160,4,256]{2,0,1:T(8,128)(2,1)} %bitcast.128), calls=%async_computation | async-start | bytes 655360 | tf_op jit(solution)/shard_map/all_to_all | solution.py:77
  33.0 205.2 %all-gather.18.cloned.1.call-start = ((), (), s32[]{:S(2)}) async-start(), calls=%async_computation.5 | async-start | bytes 1310720 | tf_op jit(solution)/shard_map/all_gather | solution.py:112
  33.0 42.2 %collective-permute-start.25 = (bf16[160,512]{1,0:T(8,128)(2,1)}, bf16[160,512]{1,0:T(8,128)(2,1)S(1)}, u32[]{:S(2)}, u32[]{:S(2)}) collective-permute-start(bf16[160,512]{1,0:T(8,128)(2,1)} %param.8), channel_id=1, source_target_pairs={{0,192},{1,193},{2,194},{3,195},{4,196},{5,197},{6,198},{7,199},{8... | collective-permute-start | bytes 491528 | tf_op jit(solution)/shard_map/ppermute | solution.py:44
  36.3 53.0 %collective-permute-start.23 = (bf16[160,512]{1,0:T(8,128)(2,1)}, bf16[160,512]{1,0:T(8,128)(2,1)S(1)}, u32[]{:S(2)}, u32[]{:S(2)}) collective-permute-start(bf16[160,512]{1,0:T(8,128)(2,1)} %param.8), channel_id=1, source_target_pairs={{0,128},{1,129},{2,130},{3,131},{4,132},{5,133},{6,134},{7,135},{8... | collective-permute-start | bytes 491528 | tf_op jit(solution)/shard_map/ppermute | solution.py:44
  36.3 68.5 %collective-permute-start.21 = (bf16[160,512]{1,0:T(8,128)(2,1)}, bf16[160,512]{1,0:T(8,128)(2,1)S(1)}, u32[]{:S(2)}, u32[]{:S(2)}) collective-permute-start(bf16[160,512]{1,0:T(8,128)(2,1)} %param.8), channel_id=1, source_target_pairs={{0,64},{1,65},{2,66},{3,67},{4,68},{5,69},{6,70},{7,71},{8,72},{9,... | collective-permute-start | bytes 491528 | tf_op jit(solution)/shard_map/ppermute | solution.py:44
  40.0 34.3 %collective-permute-start.15 = (bf16[640,256]{1,0:T(8,128)(2,1)S(1)}, bf16[640,256]{1,0:T(8,128)(2,1)S(1)}, u32[]{:S(2)}, u32[]{:S(2)}) collective-permute-start(bf16[640,256]{1,0:T(8,128)(2,1)S(1)} %bitcast.143), channel_id=1, source_target_pairs={{0,4},{1,5},{2,6},{3,7},{4,0},{5,1},{6,2},{7,3},{8,12},{9,13},{10,... | collective-permute-start | bytes 983048 | tf_op jit(solution)/shard_map/ppermute | solution.py:44
  47.6 71.5 %collective-permute-start.6 = (bf16[256,512]{1,0:T(8,128)(2,1)}, bf16[256,512]{1,0:T(8,128)(2,1)S(1)}, u32[]{:S(2)}, u32[]{:S(2)}) collective-permute-start(bf16[256,512]{1,0:T(8,128)(2,1)} %constant_dynamic-slice_fusion), channel_id=1, source_target_pairs={{0,0},{1,1},{2,2},{3,3},{4,32},{5,33},{6,34},{7,35},{8,64},{9,65},... | collective-permute-start | bytes 786440 | tf_op jit(solution)/shard_map/ppermute | solution.py:44
  74.3 62.9 %collective-permute-start.20 = (bf16[640,512]{1,0:T(8,128)(2,1)S(1)}, bf16[640,512]{1,0:T(8,128)(2,1)}, u32[]{:S(2)}, u32[]{:S(2)}) collective-permute-start(bf16[640,512]{1,0:T(8,128)(2,1)S(1)} %all_gather.44), channel_id=1, source_target_pairs={{0,32},{1,33},{2,34},{3,35},{4,36},{5,37},{6,38},{7,39},{8,40},{9,... | collective-permute-start | bytes 1966088 | tf_op jit(solution)/shard_map/ppermute | solution.py:44
  75.2 44.7 %collective-permute-start.18 = (bf16[2,640,256]{2,1,0:T(8,128)(2,1)}, bf16[2,640,256]{2,1,0:T(8,128)(2,1)}, u32[]{:S(2)}, u32[]{:S(2)}) collective-permute-start(bf16[2,640,256]{2,1,0:T(8,128)(2,1)} %maximum_select_fusion.3), channel_id=1, source_target_pairs={{0,24},{1,25},{2,26},{3,27},{4,28},{5,29},{6,30},{7,31},{8,0},{9,1... | collective-permute-start | bytes 1966088 | tf_op jit(solution)/shard_map/ppermute | solution.py:44
  89.3 32.1 %collective-permute-start.16 = (bf16[2,640,256]{2,1,0:T(8,128)(2,1)}, bf16[2,640,256]{2,1,0:T(8,128)(2,1)}, u32[]{:S(2)}, u32[]{:S(2)}) collective-permute-start(bf16[2,640,256]{2,1,0:T(8,128)(2,1)} %maximum_select_fusion.3), channel_id=1, source_target_pairs={{0,8},{1,9},{2,10},{3,11},{4,12},{5,13},{6,14},{7,15},{8,16},{9,17... | collective-permute-start | bytes 1966088 | tf_op jit(solution)/shard_map/ppermute | solution.py:44
  104.8 0.7 copy-start.24
  105.5 28.3 %collective-permute-start.26 = (bf16[640,512]{1,0:T(8,128)(2,1)S(1)}, bf16[640,512]{1,0:T(8,128)(2,1)}, u32[]{:S(2)}, u32[]{:S(2)}) collective-permute-start(bf16[640,512]{1,0:T(8,128)(2,1)S(1)} %all_gather.47), channel_id=1, source_target_pairs={{0,32},{1,33},{2,34},{3,35},{4,36},{5,37},{6,38},{7,39},{8,40},{9,... | collective-permute-start | bytes 1966088 | tf_op jit(solution)/shard_map/ppermute | solution.py:44
  119.2 0.7 copy-start.14
  119.2 16.1 %collective-permute-start.24 = (bf16[640,512]{1,0:T(8,128)(2,1)S(1)}, bf16[640,512]{1,0:T(8,128)(2,1)}, u32[]{:S(2)}, u32[]{:S(2)}) collective-permute-start(bf16[640,512]{1,0:T(8,128)(2,1)S(1)} %all_gather.46), channel_id=1, source_target_pairs={{0,32},{1,33},{2,34},{3,35},{4,36},{5,37},{6,38},{7,39},{8,40},{9,... | collective-permute-start | bytes 1966088 | tf_op jit(solution)/shard_map/ppermute | solution.py:44
  119.9 140.8 %all-gather.10.cloned.1.call-start = ((), (), s32[]{:S(2)}) async-start(), calls=%async_computation.1 | async-start | bytes 1310720 | tf_op jit(solution)/shard_map/all_gather | solution.py:107
  121.0 9.6 %collective-permute-start.19 = (bf16[640,256]{1,0:T(8,128)(2,1)S(1)}, bf16[640,256]{1,0:T(8,128)(2,1)S(1)}, u32[]{:S(2)}, u32[]{:S(2)}) collective-permute-start(bf16[640,256]{1,0:T(8,128)(2,1)S(1)} %slice_bitcast_fusion.2), channel_id=1, source_target_pairs={{0,24},{1,25},{2,26},{3,27},{4,28},{5,29},{6,30},{7,31},{8,0},{9,1... | collective-permute-start | bytes 983048 | tf_op jit(solution)/shard_map/ppermute | solution.py:44
  122.3 9.4 %collective-permute-start.17 = (bf16[640,256]{1,0:T(8,128)(2,1)S(1)}, bf16[640,256]{1,0:T(8,128)(2,1)S(1)}, u32[]{:S(2)}, u32[]{:S(2)}) collective-permute-start(bf16[640,256]{1,0:T(8,128)(2,1)S(1)} %slice_bitcast_fusion.3), channel_id=1, source_target_pairs={{0,8},{1,9},{2,10},{3,11},{4,12},{5,13},{6,14},{7,15},{8,16},{9,17... | collective-permute-start | bytes 983048 | tf_op jit(solution)/shard_map/ppermute | solution.py:44
  130.5 6.3 %collective-permute-start.22 = (bf16[640,512]{1,0:T(8,128)(2,1)S(1)}, bf16[640,512]{1,0:T(8,128)(2,1)S(1)}, u32[]{:S(2)}, u32[]{:S(2)}) collective-permute-start(bf16[640,512]{1,0:T(8,128)(2,1)S(1)} %all_gather.45), channel_id=1, source_target_pairs={{0,32},{1,33},{2,34},{3,35},{4,36},{5,37},{6,38},{7,39},{8,40},{9,... | collective-permute-start | bytes 1966088 | tf_op jit(solution)/shard_map/ppermute | solution.py:44
  136.8 2.4 copy-start.17
  136.8 2.4 copy-start.18
  136.8 2.4 copy-start.19
  139.2 2.3 copy-start.2
  139.2 2.3 copy-start.15
  141.4 41.1 %copy-start.23 = (bf16[160,1024]{1,0:T(8,128)(2,1)S(1)}, bf16[160,1024]{1,0:T(8,128)(2,1)}, u32[]{:S(2)}) copy-start(bf16[160,1024]{1,0:T(8,128)(2,1)} %param.6) | copy-start | bytes 983044
  141.4 41.1 %copy-start.16 = (bf16[160,512]{1,0:T(8,128)(2,1)S(1)}, bf16[160,512]{1,0:T(8,128)(2,1)}, u32[]{:S(2)}) copy-start(bf16[160,512]{1,0:T(8,128)(2,1)} %param.8) | copy-start | bytes 491524
  141.4 119.3 %all-gather.14.cloned.1.call-start = ((), (), s32[]{:S(2)}) async-start(), calls=%async_computation.3 | async-start | bytes 2621440 | tf_op jit(solution)/shard_map/all_gather | solution.py:112
  142.4 24.0 %collective-permute-start.9 = (bf16[2,256,512]{2,1,0:T(8,128)(2,1)}, bf16[2,256,512]{2,1,0:T(8,128)(2,1)S(1)}, u32[]{:S(2)}, u32[]{:S(2)}) collective-permute-start(bf16[2,256,512]{2,1,0:T(8,128)(2,1)} %pad_maximum_fusion), channel_id=1, source_target_pairs={{0,128},{1,129},{2,130},{3,131},{4,132},{5,133},{6,134},{7,135},{8... | collective-permute-start | bytes 1572872 | tf_op jit(solution)/shard_map/ppermute | solution.py:44
  166.4 0.8 copy-start.20
  167.3 93.5 %all-gather.16.cloned.1.call-start = ((), (), s32[]{:S(2)}) async-start(), calls=%async_computation.4 | async-start | bytes 2621440 | tf_op jit(solution)/shard_map/all_gather | solution.py:112
  167.3 14.2 %collective-permute-start.11 = (bf16[2,256,512]{2,1,0:T(8,128)(2,1)}, bf16[2,256,512]{2,1,0:T(8,128)(2,1)S(1)}, u32[]{:S(2)}, u32[]{:S(2)}) collective-permute-start(bf16[2,256,512]{2,1,0:T(8,128)(2,1)} %pad_maximum_fusion), channel_id=1, source_target_pairs={{0,192},{1,193},{2,194},{3,195},{4,196},{5,197},{6,198},{7,199},{8... | collective-permute-start | bytes 1572872 | tf_op jit(solution)/shard_map/ppermute | solution.py:44
  181.5 0.8 copy-start.21
  182.4 95.9 %all-gather.12.cloned.1.call-start = ((), (), s32[]{:S(2)}) async-start(), calls=%async_computation.2 | async-start | bytes 2621440 | tf_op jit(solution)/shard_map/all_gather | solution.py:112
  182.5 27.1 %collective-permute-start = (bf16[160,1536]{1,0:T(8,128)(2,1)S(1)}, bf16[160,1536]{1,0:T(8,128)(2,1)S(1)}, u32[]{:S(2)}, u32[]{:S(2)}) collective-permute-start(bf16[160,1536]{1,0:T(8,128)(2,1)S(1)} %constant_dynamic-update-slice_fusion), channel_id=1, source_target_pairs={{0,4},{1,5},{2,6},{3,7},{4,0},{5,1},{6,2},{7,3},{8,12},{9,13},{10,... | collective-permute-start | bytes 1474568 | tf_op jit(solution)/shard_map/ppermute | solution.py:44
  210.7 22.8 %collective-permute-start.3 = (bf16[2,160,1536]{2,1,0:T(8,128)(2,1)}, bf16[2,160,1536]{2,1,0:T(8,128)(2,1)S(1)}, u32[]{:S(2)}, u32[]{:S(2)}) collective-permute-start(bf16[2,160,1536]{2,1,0:T(8,128)(2,1)} %maximum_select_fusion.1), channel_id=1, source_target_pairs={{0,24},{1,25},{2,26},{3,27},{4,28},{5,29},{6,30},{7,31},{8,0},{9,1... | collective-permute-start | bytes 2949128 | tf_op jit(solution)/shard_map/ppermute | solution.py:44
  212.5 14.0 %collective-permute-start.7 = (bf16[2,256,512]{2,1,0:T(8,128)(2,1)}, bf16[2,256,512]{2,1,0:T(8,128)(2,1)S(1)}, u32[]{:S(2)}, u32[]{:S(2)}) collective-permute-start(bf16[2,256,512]{2,1,0:T(8,128)(2,1)} %pad_maximum_fusion), channel_id=1, source_target_pairs={{0,64},{1,65},{2,66},{3,67},{4,68},{5,69},{6,70},{7,71},{8,72},{9,... | collective-permute-start | bytes 1572872 | tf_op jit(solution)/shard_map/ppermute | solution.py:44
  212.8 22.9 %collective-permute-start.1 = (bf16[2,160,1536]{2,1,0:T(8,128)(2,1)}, bf16[2,160,1536]{2,1,0:T(8,128)(2,1)S(1)}, u32[]{:S(2)}, u32[]{:S(2)}) collective-permute-start(bf16[2,160,1536]{2,1,0:T(8,128)(2,1)} %maximum_select_fusion.1), channel_id=1, source_target_pairs={{0,8},{1,9},{2,10},{3,11},{4,12},{5,13},{6,14},{7,15},{8,16},{9,17... | collective-permute-start | bytes 2949128 | tf_op jit(solution)/shard_map/ppermute | solution.py:44
  212.8 44.5 %collective-permute-start.5 = (bf16[1024,512]{1,0:T(8,128)(2,1)S(1)}, bf16[1024,512]{1,0:T(8,128)(2,1)}, u32[]{:S(2)}, u32[]{:S(2)}) collective-permute-start(bf16[1024,512]{1,0:T(8,128)(2,1)S(1)} %copy-done.2), channel_id=1, source_target_pairs={{0,32},{1,33},{2,34},{3,35},{4,36},{5,37},{6,38},{7,39},{8,40},{9,... | collective-permute-start | bytes 3145736 | tf_op jit(solution)/shard_map/ppermute | solution.py:44
  226.5 0.8 copy-start.22
  234.3 12.6 %collective-permute-start.4 = (bf16[160,1536]{1,0:T(8,128)(2,1)}, bf16[160,1536]{1,0:T(8,128)(2,1)}, u32[]{:S(2)}, u32[]{:S(2)}) collective-permute-start(bf16[160,1536]{1,0:T(8,128)(2,1)} %slice_bitcast_fusion), channel_id=1, source_target_pairs={{0,24},{1,25},{2,26},{3,27},{4,28},{5,29},{6,30},{7,31},{8,0},{9,1... | collective-permute-start | bytes 1474568 | tf_op jit(solution)/shard_map/ppermute | solution.py:44
  236.5 13.4 %collective-permute-start.2 = (bf16[160,1536]{1,0:T(8,128)(2,1)}, bf16[160,1536]{1,0:T(8,128)(2,1)}, u32[]{:S(2)}, u32[]{:S(2)}) collective-permute-start(bf16[160,1536]{1,0:T(8,128)(2,1)} %slice_bitcast_fusion.1), channel_id=1, source_target_pairs={{0,8},{1,9},{2,10},{3,11},{4,12},{5,13},{6,14},{7,15},{8,16},{9,17... | collective-permute-start | bytes 1474568 | tf_op jit(solution)/shard_map/ppermute | solution.py:44
  238.2 21.1 %collective-permute-start.13 = (bf16[1024,512]{1,0:T(8,128)(2,1)}, bf16[1024,512]{1,0:T(8,128)(2,1)S(1)}, u32[]{:S(2)}, u32[]{:S(2)}) collective-permute-start(bf16[1024,512]{1,0:T(8,128)(2,1)} %all-gather.18.cloned.1.call-done), channel_id=1, source_target_pairs={{0,32},{1,33},{2,34},{3,35},{4,36},{5,37},{6,38},{7,39},{8,40},{9,... | collective-permute-start | bytes 3145736 | tf_op jit(solution)/shard_map/ppermute | solution.py:44
  256.9 0.8 copy-start.9
  260.7 25.8 %collective-permute-start.10 = (bf16[4,2,256,512]{3,2,1,0:T(8,128)(2,1)}, bf16[4,2,256,512]{3,2,1,0:T(8,128)(2,1)}, u32[]{:S(2)}, u32[]{:S(2)}) collective-permute-start(bf16[4,2,256,512]{3,2,1,0:T(8,128)(2,1)} %bitcast.146), channel_id=1, source_target_pairs={{0,32},{1,33},{2,34},{3,35},{4,36},{5,37},{6,38},{7,39},{8,40},{9,... | collective-permute-start | bytes 6291464 | tf_op jit(solution)/shard_map/ppermute | solution.py:44
  260.7 3.3 %copy-start.3 = (bf16[8,256,512]{2,1,0:T(8,128)(2,1)S(1)}, bf16[8,256,512]{2,1,0:T(8,128)(2,1)}, u32[]{:S(2)}) copy-start(bf16[8,256,512]{2,1,0:T(8,128)(2,1)} %all-gather.14.cloned.1.call-done) | copy-start | bytes 6291460
  260.7 28.0 %collective-permute-start.12 = (bf16[4,2,256,512]{3,2,1,0:T(8,128)(2,1)}, bf16[4,2,256,512]{3,2,1,0:T(8,128)(2,1)}, u32[]{:S(2)}, u32[]{:S(2)}) collective-permute-start(bf16[4,2,256,512]{3,2,1,0:T(8,128)(2,1)} %bitcast.148), channel_id=1, source_target_pairs={{0,32},{1,33},{2,34},{3,35},{4,36},{5,37},{6,38},{7,39},{8,40},{9,... | collective-permute-start | bytes 6291464 | tf_op jit(solution)/shard_map/ppermute | solution.py:44
  278.3 3.0 copy-start
  278.3 3.0 copy-start.11
  278.3 6.9 %collective-permute-start.8 = (bf16[4,2,256,512]{3,2,1,0:T(8,128)(2,1)}, bf16[4,2,256,512]{3,2,1,0:T(8,128)(2,1)S(1)}, u32[]{:S(2)}, u32[]{:S(2)}) collective-permute-start(bf16[4,2,256,512]{3,2,1,0:T(8,128)(2,1)} %bitcast.150), channel_id=1, source_target_pairs={{0,32},{1,33},{2,34},{3,35},{4,36},{5,37},{6,38},{7,39},{8,40},{9,... | collective-permute-start | bytes 6291464 | tf_op jit(solution)/shard_map/ppermute | solution.py:44
  278.3 3.3 %copy-start.4 = (bf16[8,256,512]{2,1,0:T(8,128)(2,1)S(1)}, bf16[8,256,512]{2,1,0:T(8,128)(2,1)}, u32[]{:S(2)}) copy-start(bf16[8,256,512]{2,1,0:T(8,128)(2,1)} %all-gather.12.cloned.1.call-done) | copy-start | bytes 6291460
  281.3 1.0 copy-start.10
  281.6 1.1 copy-start.8
  282.3 1.2 copy-start.1
  282.3 1.5 copy-start.12
  285.1 1.0 copy-start.7
  286.5 1.8 copy-start.6
  288.7 1.8 copy-start.5
  292.1 1.7 copy-start.13
Sparse Core Ops, SparseCore 0:
  120.0 23.5 all-gather.17
  145.5 26.8 all-gather.9
  174.2 33.7 all-gather.13
  209.6 33.4 all-gather.15
  244.8 33.4 all-gather.11
